TPU v7x, 512 devices: a whole 4x4x16 slice. The times are simulated.
512 devices in a mesh: dp: 64 (over z, y_hi, core), mp: 8 (over x, y_lo).
Axes of the slice: x: 4, y: 4 (y_hi: 2, y_lo: 2; y = y_hi * 2 + y_lo), z: 16, core: 2. Of those that a mesh axis runs over, the one named last changes fastest.
Arguments:
- acts: bfloat16 [32768, 8192], P('dp', 'mp'), may hold values from -6 to 6
- out_grads: bfloat16 [32768, 14336], P('dp', 'mp'), may hold values from -0.09375 to 0.09375
- basis: bfloat16 [8192, 512], P('mp'), may hold values from -0.0625 to 0.0625
- weights: bfloat16 [14336, 8192], P(('mp', 'dp')), may hold values from -0.59765625 to 0.59765625
- first_moment: float32 [14336, 512], P(('mp', 'dp')), may hold values from -2 to 2
- second_moment: float32 [14336, 512], P(('mp', 'dp')), may hold values from 0.05 to 1
Outputs:
- new_weights: bfloat16 [14336, 8192], P(('mp', 'dp'))
- moment_new: float32 [14336, 512], P(('mp', 'dp'))
- second_new: float32 [14336, 512], P(('mp', 'dp'))
All inputs are finite; a program needn't handle non-finite values.
Results may differ from a plain program's by a relative error of at most 0.01.
Values may be sent and summed in bfloat16 or wider, within the bound.
A program may use at most 64 MiB of HBM per device.

v0:
```python
import jax
import jax.numpy as jnp
from jax import lax
from jax.sharding import PartitionSpec as P

beta_one = 0.9
beta_two = 0.99
corr_one = 1.0 - 0.9**10
corr_two = 1.0 - 0.99**10
adam_eps = 1e-08
step_size = 1.0


def on_device(acts, out_grads, basis, weights, first_moment, second_moment):
    partial_proj = jnp.dot(acts, basis, preferred_element_type=jnp.float32)
    projected = lax.psum(partial_proj, "mp").astype(jnp.bfloat16)
    terms = lax.dot_general(
        out_grads, projected, (((0,), (0,)), ((), ())), preferred_element_type=jnp.float32
    )
    low_grad = lax.psum_scatter(terms, "dp", scatter_dimension=0, tiled=True)
    moment_new = beta_one * first_moment + (1.0 - beta_one) * low_grad
    second_new = beta_two * second_moment + (1.0 - beta_two) * low_grad * low_grad
    direction = (moment_new / corr_one / (jnp.sqrt(second_new / corr_two) + adam_eps)).astype(
        jnp.bfloat16
    )
    stacked = lax.all_gather(direction, "mp", axis=0, tiled=True)
    blocks = lax.dot_general(
        stacked, basis, (((1,), (1,)), ((), ())), preferred_element_type=jnp.float32
    )
    delta = lax.all_to_all(
        blocks.astype(jnp.bfloat16), "mp", split_axis=0, concat_axis=1, tiled=True
    ).astype(blocks.dtype)
    new_weights = (weights.astype(jnp.float32) - step_size * delta).astype(jnp.bfloat16)
    return (new_weights, moment_new, second_new)


def solution(mesh):
    return jax.shard_map(
        on_device,
        mesh=mesh,
        in_specs=(
            P("dp", "mp"),
            P("dp", "mp"),
            P("mp", None),
            P(("mp", "dp"), None),
            P(("mp", "dp"), None),
            P(("mp", "dp"), None),
        ),
        out_specs=(P(("mp", "dp"), None), P(("mp", "dp"), None), P(("mp", "dp"), None)),
        check_vma=False,
    )
```

profile of v0, /device:TPU:1, one launch (start us, length us, event | category | flops | bytes accessed | tf_op | source)
XLA Modules:
  0.0 669.9 jit_solution(12167605154687932565)
XLA Ops:
  7.2 0.0 copy-start
  7.2 0.0 all-reduce.4.cloned.1.call-start
  7.2 2.4 fusion.4
  9.6 57.5 %all-reduce.5 = bf16[512,512]{1,0:T(8,128)(2,1)S(1)} all-reduce(f32[512,512]{1,0:T(8,128)S(1)} %fusion.4), channel_id=1, replica_groups=mesh['dp'=64,'mp'=8] {'mp'}, use_global_device_ids=true, to_apply=%region_0.0 | all-reduce | flops 262144 | bytes 1572864 | tf_op jit(solution)/shard_map/psum | solution.py:16
  67.1 0.0 copy-done
  67.1 3.0 convolution_bitcast_fusion
  70.1 0.0 copy-start.2
  70.1 0.0 copy-start.3
  70.1 0.0 all-reduce.4.cloned.1.call-update
  70.1 1.3 dynamic-slice
  72.0 552.1 %all-reduce.4.cloned.1.call-done = f32[1792,512]{0,1:T(8,128)} async-done(((f32[1792,512]{0,1:T(8,128)}), f32[1792,512]{0,1:T(8,128)}) %all-reduce.4.cloned.1.call-update) | async-done | bytes 3670032
  624.1 1.2 constant_dynamic-slice_fusion
  625.3 0.1 copy.31
  625.4 0.0 copy-done.2
  625.4 0.0 copy-done.3
  625.4 0.7 fusion.2
  626.1 22.3 %all-gather = bf16[8,28,512]{2,1,0:T(8,128)(2,1)S(1)} all-gather(bf16[1,28,512]{2,1,0:T(8,128)(2,1)S(1)} %get-tuple-element.15), channel_id=1, replica_groups=mesh['dp'=64,'mp'=8] {'mp'}, dimensions={0}, use_global_device_ids=true | all-gather | bytes 258048 | tf_op jit(solution)/shard_map/all_gather | solution.py:26
  648.5 1.7 convolution_convert_fusion
  650.2 0.1 all_to_all.10
  650.3 10.4 %all_to_all.13 = bf16[8,28,1024]{2,1,0:T(8,128)(2,1)S(1)} all-to-all(bf16[8,28,1024]{2,1,0:T(8,128)(2,1)S(1)} %all_to_all.10), channel_id=1, replica_groups=mesh['dp'=64,'mp'=8] {'mp'}, dimensions={0} | all-to-all | bytes 917504 | tf_op jit(solution)/shard_map/all_to_all | solution.py:30
  660.8 0.0 copy-start.1
  660.8 0.1 convert_bitcast_fusion
  660.9 0.5 copy.34
  661.4 0.1 pad
  661.5 0.6 copy.37
  662.1 0.0 copy-done.1
  662.2 0.9 subtract_convert_fusion
  (1 shorter events, 0.0 us)
Async XLA Ops:
  7.2 59.9 %copy-start = (bf16[512,1792]{1,0:T(8,128)(2,1)S(1)}, bf16[512,1792]{1,0:T(8,128)(2,1)}, u32[]{:S(2)}) copy-start(bf16[512,1792]{1,0:T(8,128)(2,1)} %param.7) | copy-start | bytes 5505028
  7.2 617.0 %all-reduce.4.cloned.1.call-start = ((), (), s32[]{:S(2)}) async-start(), calls=%async_computation.1 | async-start | bytes 7340032
  70.1 555.4 %copy-start.2 = (f32[28,512]{1,0:T(8,128)S(1)}, f32[28,512]{1,0:T(8,128)}, u32[]{:S(2)}) copy-start(f32[28,512]{1,0:T(8,128)} %param.10) | copy-start | bytes 172036
  70.1 555.4 %copy-start.3 = (f32[28,512]{1,0:T(8,128)S(1)}, f32[28,512]{1,0:T(8,128)}, u32[]{:S(2)}) copy-start(f32[28,512]{1,0:T(8,128)} %param.11) | copy-start | bytes 172036
  660.8 1.4 copy-start.1
Sparse Core Ops, SparseCore 0:
  70.2 553.8 all-reduce.3
where the time goes:
time: 677 us; the launch traced here: 670 us
  waiting for transfers between devices  552 us (82%)
  blocking collectives  90.2 us (13%)
  between operations  14.8 us (2%)
  matrix products  7.06 us (1%)
    unnamed x2, waiting for transfers between devices  552 us
    psum x1, blocking collectives, on_device(): projected = lax.psum(partial_proj, 'mp').astype(jnp.bfloat16)  57.5 us
    all_gather x1, blocking collectives, on_device(): stacked = lax.all_gather(direction, 'mp', axis=0, tiled=True)  22.3 us
  transfers between devices with their start and end apart: 1, of which 1 were waited for; matrix products, arithmetic and copies ran while one was open for 0% of the time, Pallas kernels for 0%

commit v1 on v0

v1 whole, which is shorter than its diff:
```python
import functools

import jax
import jax.numpy as jnp
from jax import lax
from jax.experimental import pallas as pl
from jax.experimental.pallas import tpu as pltpu
from jax.sharding import PartitionSpec as P

beta_one = 0.9
beta_two = 0.99
corr_one = 1.0 - 0.9**10
corr_two = 1.0 - 0.99**10
adam_eps = 1e-08
step_size = 1.0

MESH = pl.DeviceIdType.MESH
F32 = jnp.float32
BF16 = jnp.bfloat16


def kernel(
    nz, nx, pad,
    acts_hbm, grads_hbm, basis_hbm, weights_hbm, first_hbm, second_hbm,
    weights_out, first_out, second_out,
    acts, grads, basis, weights, first, second,
    part, part_in, proj, turned,
    quarters, sibling_in, down_out, down_in, up_out, up_in,
    column, fin_out, fin_in, dirs, blocks, delta,
    load_sem, rs_send, rs_recv, ag_send, ag_recv, core_send, core_recv,
    down_send, down_recv, up_send, up_recv, fin_send, fin_recv,
    dir_send, dir_recv, blk_send, blk_recv,
):
    dp, mp = lax.axis_index("dp"), lax.axis_index("mp")
    z, y_hi, core = dp // 4, (dp // 2) % 2, dp % 2
    x, y_lo = mp // 2, mp % 2
    tokens, width = acts.shape
    hidden = turned.shape[0]
    rank = basis.shape[1]
    rows = first.shape[0]
    span = hidden // nz
    piece = tokens // (2 * nx)

    def dp_of(z_at, y_at, core_at):
        return (z_at % nz) * 4 + y_at * 2 + core_at

    def mp_of(r, dy):
        return ((x + r + nx) % nx) * 2 + (y_lo + dy) % 2

    loads = [
        pltpu.make_async_copy(src, dst, load_sem.at[i])
        for i, (src, dst) in enumerate(
            (
                (basis_hbm, basis),
                (acts_hbm, acts),
                (grads_hbm, grads),
                (weights_hbm, weights),
                (first_hbm, first),
                (second_hbm, second),
            )
        )
    ]
    for load in loads:
        load.start()

    relations = [(r, dy) for r in range(nx) for dy in range(2)]
    peers = [({"mp": mp_of(r, dy)}) for r, dy in relations[1:]]
    peers += [
        {"dp": dp_of(z, y_hi, 1 - core)},
        {"dp": dp_of(z + nz - 1, y_hi, core)},
        {"dp": dp_of(z + 1, y_hi, core)},
        {"dp": dp_of(z, 1 - y_hi, core)},
        {"dp": dp_of(z, 1 - y_hi, 1 - core)},
    ]
    barrier = pltpu.get_barrier_semaphore()
    for peer in peers:
        pl.semaphore_signal(barrier, inc=1, device_id=peer, device_id_type=MESH)

    def send(src, dst, send_sem, recv_sem, device):
        copy = pltpu.make_async_remote_copy(
            src_ref=src, dst_ref=dst, send_sem=send_sem, recv_sem=recv_sem,
            device_id=device, device_id_type=MESH,
        )
        copy.start()
        return copy

    loads[0].wait()
    loads[1].wait()

    def project(r):
        x_at = (x + r) % nx
        at = pl.multiple_of(x_at * 2 * piece, 2 * piece)
        value = jnp.dot(acts[pl.ds(at, 2 * piece), :], basis[...], preferred_element_type=F32)
        part[pl.ds(at, 2 * piece), :] = value.astype(BF16)

    def piece_of(ref, index):
        return ref.at[pl.ds(pl.multiple_of(index * piece, piece), piece), :]

    order = [nx // 2] + [r for r in range(1, nx) if r != nx // 2] + [0]
    rs = {}
    for n, r in enumerate(order):
        project(r)
        if n == 0:
            pl.semaphore_wait(barrier, len(peers))
        for dy in range(2):
            q = 2 * r + dy
            if q:
                rs[q] = send(
                    piece_of(part, mp_of(r, dy)), part_in.at[q],
                    rs_send.at[q], rs_recv.at[q], {"mp": mp_of(r, dy)},
                )

    loads[2].wait()
    for b in range(hidden // 128):
        turned[pl.ds(b * 128, 128), :] = grads[:, pl.ds(b * 128, 128)].T

    total = part[pl.ds(pl.multiple_of(mp * piece, piece), piece), :].astype(F32)
    for q in range(1, 2 * nx):
        rs[q].wait()
        total = total + part_in[q].astype(F32)
    proj[pl.ds(pl.multiple_of(mp * piece, piece), piece), :] = total.astype(BF16)
    ag = []
    for q, (r, dy) in enumerate(relations):
        if q:
            ag.append(
                send(
                    piece_of(proj, mp), piece_of(proj, mp),
                    ag_send.at[q], ag_recv.at[q], {"mp": mp_of(r, dy)},
                )
            )
    for copy in ag:
        copy.wait()

    half = nz // 2
    schedule = [(-half, "down", 0)]
    for k in range(half - 1):
        schedule.append((-(half - 1 - k), "down", k + 1))
        schedule.append((half - 1 - k, "up", k))
    schedule.append((0, "own", 0))
    siblings = [None] * len(schedule)

    def multiply(n):
        at = (z + schedule[n][0] + nz) % nz
        value = jnp.dot(
            turned[pl.ds(pl.multiple_of(at * span, 16), span), :], proj[...],
            preferred_element_type=F32,
        ).astype(BF16)
        for i in range(4):
            quarters[n, i] = value[:, i * (rank // 4) : (i + 1) * (rank // 4)]
        siblings[n] = send(
            quarters.at[n, pl.ds(2 * (1 - core), 2)], sibling_in.at[n],
            core_send.at[n], core_recv.at[n], {"dp": dp_of(z, y_hi, 1 - core)},
        )

    ring = {}
    ahead = 4
    for n in range(min(ahead, len(schedule))):
        multiply(n)
    for n, (_, way, k) in enumerate(schedule):
        siblings[n].wait()
        for s in range(2):
            value = quarters[n, 2 * core + s].astype(F32) + sibling_in[n, s].astype(F32)
            if way == "own":
                ring["down", half - 1, s].wait()
                ring["up", half - 2, s].wait()
                value = value + down_in[half - 1, s].astype(F32) + up_in[half - 2, s].astype(F32)
                column[pl.ds(0, span), pl.ds(s * 128, 128)] = value
                continue
            out, into, sent, received, towards = (
                (up_out, up_in, up_send, up_recv, z + 1)
                if way == "up"
                else (down_out, down_in, down_send, down_recv, z + nz - 1)
            )
            if k:
                ring[way, k - 1, s].wait()
                value = value + into[k - 1, s].astype(F32)
            out[k, s] = value.astype(BF16)
            ring[way, k, s] = send(
                out.at[k, s], into.at[k, s], sent.at[k, s], received.at[k, s],
                {"dp": dp_of(towards, y_hi, core)},
            )
        if n + ahead < len(schedule):
            multiply(n + ahead)

    column[pl.ds(span, 8), :] = jnp.zeros((8, rank // 2), F32)
    here = y_hi * 2 + core
    for b in range(4):
        for s in range(2):
            fin_out[b, s] = column[pl.ds(b * rows, pad), pl.ds(s * 128, 128)].astype(BF16)
    fin = []
    for i, (dy, dc) in enumerate(((1, 0), (1, 1), (0, 1))):
        y_at, core_at = (y_hi + dy) % 2, (core + dc) % 2
        fin.append(
            send(
                fin_out.at[y_at * 2 + core_at], fin_in.at[here],
                fin_send.at[i], fin_recv.at[i], {"dp": dp_of(z, y_at, core_at)},
            )
        )
    fin_in[here] = fin_out[here]
    for load in loads[3:]:
        load.wait()
    for copy in fin:
        copy.wait()

    for c in range(2):
        for s in range(2):
            low_grad = (fin_in[c, s].astype(F32) + fin_in[2 + c, s].astype(F32))[:rows]
            cut = pl.ds((2 * c + s) * 128, 128)
            moment_new = beta_one * first[:, cut] + (1.0 - beta_one) * low_grad
            second_new = beta_two * second[:, cut] + (1.0 - beta_two) * low_grad * low_grad
            direction = moment_new / corr_one / (jnp.sqrt(second_new / corr_two) + adam_eps)
            first_out[:, cut] = moment_new
            second_out[:, cut] = second_new
            padded = jnp.concatenate([direction, jnp.zeros((pad - rows, 128), F32)], axis=0)
            dirs[0, :, cut] = padded.astype(BF16)

    gathered = {}
    for q, (r, dy) in enumerate(relations):
        if q:
            gathered[q] = send(
                dirs.at[0], dirs.at[q], dir_send.at[q], dir_recv.at[q], {"mp": mp_of(r, dy)},
            )
    for copy in gathered.values():
        copy.wait()
    stacked = dirs[...].reshape(2 * nx * pad, rank)
    product = lax.dot_general(
        stacked, basis[...], (((1,), (1,)), ((), ())), preferred_element_type=F32
    ).astype(BF16)
    returned = {}
    for q, (r, dy) in enumerate(relations):
        if q:
            blocks[q] = product[q * pad : (q + 1) * pad]
            returned[q] = send(
                blocks.at[q], delta.at[q], blk_send.at[q], blk_recv.at[q], {"mp": mp_of(-r, dy)},
            )
        else:
            delta[0] = product[:pad]
    for q, (r, dy) in enumerate(relations):
        if q:
            returned[q].wait()
        at = pl.ds(pl.multiple_of(mp_of(r, dy) * width, width), width)
        change = delta[q].astype(F32)[:rows]
        weights_out[:, at] = (weights[:, at].astype(F32) - step_size * change).astype(BF16)


def on_device(nz, nx, acts, out_grads, basis, weights, first_moment, second_moment):
    tokens, width = acts.shape
    hidden = out_grads.shape[1]
    rank = basis.shape[1]
    rows, full = weights.shape
    pad = -(-rows // 16) * 16
    span = hidden // nz
    peers = 2 * nx
    piece = tokens // peers
    half = nz // 2
    dma = pltpu.SemaphoreType.DMA
    vmem = pltpu.VMEM
    return pl.pallas_call(
        functools.partial(kernel, nz, nx, pad),
        out_shape=(
            jax.ShapeDtypeStruct(weights.shape, BF16),
            jax.ShapeDtypeStruct(first_moment.shape, F32),
            jax.ShapeDtypeStruct(second_moment.shape, F32),
        ),
        in_specs=[pl.BlockSpec(memory_space=pl.ANY)] * 6,
        out_specs=[pl.BlockSpec(memory_space=pltpu.VMEM)] * 3,
        scratch_shapes=[
            vmem(acts.shape, BF16),
            vmem(out_grads.shape, BF16),
            vmem(basis.shape, BF16),
            vmem(weights.shape, BF16),
            vmem(first_moment.shape, F32),
            vmem(second_moment.shape, F32),
            vmem((tokens, rank), BF16),
            vmem((peers, piece, rank), BF16),
            vmem((tokens, rank), BF16),
            vmem((hidden, tokens), BF16),
            vmem((nz, 4, span, rank // 4), BF16),
            vmem((nz, 2, span, rank // 4), BF16),
            vmem((half, 2, span, rank // 4), BF16),
            vmem((half, 2, span, rank // 4), BF16),
            vmem((half, 2, span, rank // 4), BF16),
            vmem((half, 2, span, rank // 4), BF16),
            vmem((span + 8, rank // 2), F32),
            vmem((4, 2, pad, rank // 4), BF16),
            vmem((4, 2, pad, rank // 4), BF16),
            vmem((peers, pad, rank), BF16),
            vmem((peers, pad, width), BF16),
            vmem((peers, pad, width), BF16),
            dma((6,)),
            dma((peers,)), dma((peers,)), dma((peers,)), dma((peers,)),
            dma((nz,)), dma((nz,)),
            dma((half, 2)), dma((half, 2)), dma((half, 2)), dma((half, 2)),
            dma((3,)), dma((3,)),
            dma((peers,)), dma((peers,)), dma((peers,)), dma((peers,)),
        ],
        compiler_params=pltpu.CompilerParams(
            collective_id=0, has_side_effects=True, vmem_limit_bytes=48 * 1024 * 1024
        ),
    )(acts, out_grads, basis, weights, first_moment, second_moment)


def solution(mesh):
    nz, nx = mesh.shape["dp"] // 4, mesh.shape["mp"] // 2
    return jax.shard_map(
        functools.partial(on_device, nz, nx),
        mesh=mesh,
        in_specs=(
            P("dp", "mp"),
            P("dp", "mp"),
            P("mp", None),
            P(("mp", "dp"), None),
            P(("mp", "dp"), None),
            P(("mp", "dp"), None),
        ),
        out_specs=(P(("mp", "dp"), None), P(("mp", "dp"), None), P(("mp", "dp"), None)),
        check_vma=False,
    )
```

time: 677 us -> 87.6 us (0.13)
  waiting for transfers between devices: 552 us -> 0 us
  blocking collectives: 90.2 us -> 0 us
  Pallas kernels: 0 us -> 77.9 us
  between operations: 14.8 us -> 0.65 us
  matrix products: 7.06 us -> 0 us
    unnamed x2 -> x0, waiting for transfers between devices: 552 us -> none
    pallas_call x0 -> x1, Pallas kernels: none -> 77.9 us  [on_device(): pl.pallas_call(functools.partial(kernel, nz, nx, pad), out_shape=(jax.Sha...]
    psum x1 -> x0, blocking collectives: 57.5 us -> none  [on_device(): projected = lax.psum(partial_proj, 'mp').astype(jnp.bfloat16)]
    all_gather x1 -> x0, blocking collectives: 22.3 us -> none  [on_device(): stacked = lax.all_gather(direction, 'mp', axis=0, tiled=True)]
    all_to_all x1 -> x0, blocking collectives: 10.4 us -> none  [on_device(): lax.all_to_all(blocks.astype(jnp.bfloat16), 'mp', split_axis=0, concat_ax...]
    dot_general x3 -> x0, matrix products: 7.06 us -> none  [the longest x1 2.98 us: on_device(): lax.dot_general(out_grads, projected, (((0,), (0,)), ((), ())), preferred...]
  transfers between devices with their start and end apart: 1 -> 0, of which waited for: 1 -> 0; matrix products, arithmetic and copies ran while one was open for 0% -> 0% of each run, Pallas kernels for 0% -> 0%
where the time goes in v1:
time: 87.6 us; the launch traced here: 87.2 us
  Pallas kernels  77.9 us (89%)
  local copies, waits for them, and re-layouts  8.71 us (10%)
    pallas_call x1, Pallas kernels, on_device(): pl.pallas_call(functools.partial(kernel, nz, nx, pad), out_shape=(jax.Sha...  77.9 us
    unnamed x15, local copies, waits for them, and re-layouts  8.71 us

profile of v1, /device:TPU:1, one launch (start us, length us, event | category | flops | bytes accessed | tf_op | source)
XLA Modules:
  0.0 87.2 jit_solution(2463025253697043902)
XLA Ops:
  0.6 0.0 copy-start
  0.6 1.5 %copy-done = bf16[512,1792]{1,0:T(8,128)(2,1)S(1)} copy-done((bf16[512,1792]{1,0:T(8,128)(2,1)S(1)}, bf16[512,1792]{1,0:T(8,128)(2,1)}, u32[]{:S(2)}) %copy-start) | copy-done | bytes 1835032
  2.1 0.0 copy-start.1
  2.1 1.2 %copy-done.1 = bf16[512,1024]{1,0:T(8,128)(2,1)S(1)} copy-done((bf16[512,1024]{1,0:T(8,128)(2,1)S(1)}, bf16[512,1024]{1,0:T(8,128)(2,1)}, u32[]{:S(2)}) %copy-start.1) | copy-done | bytes 1048600
  3.4 0.0 copy-start.2
  3.4 1.2 %copy-done.2 = bf16[1024,512]{1,0:T(8,128)(2,1)S(1)} copy-done((bf16[1024,512]{1,0:T(8,128)(2,1)S(1)}, bf16[1024,512]{1,0:T(8,128)(2,1)}, u32[]{:S(2)}) %copy-start.2) | copy-done | bytes 1048600
  4.6 0.0 copy-start.3
  4.6 1.0 %copy-done.3 = bf16[28,8192]{1,0:T(8,128)(2,1)S(1)} copy-done((bf16[28,8192]{1,0:T(8,128)(2,1)S(1)}, bf16[28,8192]{1,0:T(8,128)(2,1)}, u32[]{:S(2)}) %copy-start.3) | copy-done | bytes 458776
  5.6 0.0 copy-start.4
  5.6 0.8 copy-done.4
  6.5 0.0 copy-start.5
  6.5 0.8 copy-done.5
  7.3 77.9 %shard_map.85 = (bf16[28,8192]{1,0:T(8,128)(2,1)S(1)}, f32[28,512]{1,0:T(8,128)S(1)}, f32[28,512]{1,0:T(8,128)S(1)}) custom-call(bf16[512,1024]{1,0:T(8,128)(2,1)S(1)} %copy-done.1, bf16[512,1792]{1,0:T(8,128)(2,1)S(1)} %copy-done, bf16[1024,512]{1,0:T(8,128)(2,1)S(1)} %copy-done.2, bf16[28,8192]{1,0:T(8,128)(2,1)S(1)} %copy-done.3, ...), custom_call_target="tpu_custom_call" | custom-call | tf_op jit(solution)/shard_map/pallas_call | solution.py:258
  85.2 0.8 copy.12
  86.0 0.6 copy.13
  86.6 0.6 copy.14
Async XLA Ops:
  0.6 1.5 %copy-start = (bf16[512,1792]{1,0:T(8,128)(2,1)S(1)}, bf16[512,1792]{1,0:T(8,128)(2,1)}, u32[]{:S(2)}) copy-start(bf16[512,1792]{1,0:T(8,128)(2,1)} %grads_hbm.1) | copy-start | bytes 5505028
  2.1 1.2 %copy-start.1 = (bf16[512,1024]{1,0:T(8,128)(2,1)S(1)}, bf16[512,1024]{1,0:T(8,128)(2,1)}, u32[]{:S(2)}) copy-start(bf16[512,1024]{1,0:T(8,128)(2,1)} %acts_hbm.1) | copy-start | bytes 3145732
  3.4 1.2 %copy-start.2 = (bf16[1024,512]{1,0:T(8,128)(2,1)S(1)}, bf16[1024,512]{1,0:T(8,128)(2,1)}, u32[]{:S(2)}) copy-start(bf16[1024,512]{1,0:T(8,128)(2,1)} %basis_hbm.1) | copy-start | bytes 3145732
  4.6 1.0 %copy-start.3 = (bf16[28,8192]{1,0:T(8,128)(2,1)S(1)}, bf16[28,8192]{1,0:T(8,128)(2,1)}, u32[]{:S(2)}) copy-start(bf16[28,8192]{1,0:T(8,128)(2,1)} %weights_hbm.1) | copy-start | bytes 1376260
  5.6 0.8 copy-start.4
  6.5 0.8 copy-start.5

commit v2 on v1

v2 whole, which is shorter than its diff:
```python
import functools

import jax
import jax.numpy as jnp
from jax import lax
from jax.experimental import pallas as pl
from jax.experimental.pallas import tpu as pltpu
from jax.sharding import PartitionSpec as P

beta_one = 0.9
beta_two = 0.99
corr_one = 1.0 - 0.9**10
corr_two = 1.0 - 0.99**10
adam_eps = 1e-08
step_size = 1.0

HUBS = (6, -6, 3, -3, 0)
LEAVES = {6: (8, 7, 5, 6), -6: (-7, -5, -6), 3: (4, 2, 3), -3: (-4, -2, -3), 0: (1, -1, 0)}

MESH = pl.DeviceIdType.MESH
F32 = jnp.float32
BF16 = jnp.bfloat16


def kernel(
    nz, nx, pad,
    acts_hbm, grads_hbm, basis_hbm, weights_hbm, first_hbm, second_hbm,
    weights_out, first_out, second_out,
    acts, grads, basis, weights, first, second,
    part, part_in, proj, turned,
    halves, sibling_in, leaf, hub_in, column, fin_out, fin_in, dirs, blocks, delta,
    load_sem, rs_send, rs_recv, ag_send, ag_recv, core_send, core_recv,
    hub_send, hub_recv, fin_send, fin_recv,
    dir_send, dir_recv, blk_send, blk_recv,
):
    dp, mp = lax.axis_index("dp"), lax.axis_index("mp")
    z, y_hi, core = dp // 4, (dp // 2) % 2, dp % 2
    x, y_lo = mp // 2, mp % 2
    tokens, width = acts.shape
    hidden = turned.shape[0]
    rank = basis.shape[1]
    rows = first.shape[0]
    span = hidden // nz
    piece = tokens // (2 * nx)

    def dp_of(z_at, y_at, core_at):
        return (z_at % nz) * 4 + y_at * 2 + core_at

    def mp_of(r, dy):
        return ((x + r + nx) % nx) * 2 + (y_lo + dy) % 2

    loads = [
        pltpu.make_async_copy(src, dst, load_sem.at[i])
        for i, (src, dst) in enumerate(
            (
                (basis_hbm, basis),
                (acts_hbm, acts),
                (grads_hbm, grads),
                (weights_hbm, weights),
                (first_hbm, first),
                (second_hbm, second),
            )
        )
    ]
    for load in loads:
        load.start()

    relations = [(r, dy) for r in range(nx) for dy in range(2)]
    peers = [({"mp": mp_of(r, dy)}) for r, dy in relations[1:]]
    peers += [{"dp": dp_of(z, y_hi, 1 - core)}, {"dp": dp_of(z, 1 - y_hi, core)}]
    for dz in (-2, -1, 1, 2):
        peers += [{"dp": dp_of(z + dz + nz, y_at, core)} for y_at in range(2)]
    for dz in HUBS[:-1]:
        peers += [{"dp": dp_of(z + dz + nz, y_hi, core_at)} for core_at in range(2)]
    barrier = pltpu.get_barrier_semaphore()
    for peer in peers:
        pl.semaphore_signal(barrier, inc=1, device_id=peer, device_id_type=MESH)

    def send(src, dst, send_sem, recv_sem, device):
        copy = pltpu.make_async_remote_copy(
            src_ref=src, dst_ref=dst, send_sem=send_sem, recv_sem=recv_sem,
            device_id=device, device_id_type=MESH,
        )
        copy.start()
        return copy

    loads[0].wait()
    loads[1].wait()

    def project(r):
        x_at = (x + r) % nx
        at = pl.multiple_of(x_at * 2 * piece, 2 * piece)
        value = jnp.dot(acts[pl.ds(at, 2 * piece), :], basis[...], preferred_element_type=F32)
        part[pl.ds(at, 2 * piece), :] = value.astype(BF16)

    def piece_of(ref, index):
        return ref.at[pl.ds(pl.multiple_of(index * piece, piece), piece), :]

    order = [nx // 2] * (nx > 1) + [r for r in range(1, nx) if r != nx // 2] + [0]
    rs = {}
    for n, r in enumerate(order):
        project(r)
        if n == 0:
            pl.semaphore_wait(barrier, len(peers))
        for dy in range(2):
            q = 2 * r + dy
            if q:
                rs[q] = send(
                    piece_of(part, mp_of(r, dy)), part_in.at[q],
                    rs_send.at[q], rs_recv.at[q], {"mp": mp_of(r, dy)},
                )

    loads[2].wait()
    for b in range(hidden // 128):
        turned[pl.ds(b * 128, 128), :] = grads[:, pl.ds(b * 128, 128)].T

    total = part[pl.ds(pl.multiple_of(mp * piece, piece), piece), :].astype(F32)
    for q in range(1, 2 * nx):
        rs[q].wait()
        total = total + part_in[q].astype(F32)
    proj[pl.ds(pl.multiple_of(mp * piece, piece), piece), :] = total.astype(BF16)
    ag = []
    for q, (r, dy) in enumerate(relations):
        if q:
            ag.append(
                send(
                    piece_of(proj, mp), piece_of(proj, mp),
                    ag_send.at[q], ag_recv.at[q], {"mp": mp_of(r, dy)},
                )
            )
    for copy in ag:
        copy.wait()

    schedule = [(h, o) for h in HUBS for o in LEAVES[h]]
    block = rank // 4
    siblings = [None] * len(schedule)

    def multiply(n):
        at = (z - schedule[n][1] + nz) % nz
        value = jnp.dot(
            turned[pl.ds(pl.multiple_of(at * span, 16), span), :], proj[...],
            preferred_element_type=F32,
        )
        for c in range(2):
            for y in range(2):
                two = [
                    value[y * span // 2 : (y + 1) * span // 2, i * block : (i + 1) * block]
                    for i in (2 * c, 2 * c + 1)
                ]
                halves[n, c, y] = jnp.concatenate(two, axis=0).astype(BF16)
        siblings[n] = send(
            halves.at[n, 1 - core], sibling_in.at[n],
            core_send.at[n], core_recv.at[n], {"dp": dp_of(z, y_hi, 1 - core)},
        )

    def slot(e, dy):
        return (e + 1) * 2 + dy

    to_hub = {}

    def scatter(n):
        h, o = schedule[n]
        e = o - h
        siblings[n].wait()
        for y in range(2):
            value = halves[n, core, y].astype(F32) + sibling_in[n, y].astype(F32)
            leaf[n, y] = value.astype(BF16)
        for dy in (1, 0):
            if e or dy:
                y_at = (y_hi + dy) % 2
                i = HUBS.index(h)
                to_hub[h, e, dy] = send(
                    leaf.at[n, y_at], hub_in.at[i, slot(e, dy)],
                    hub_send.at[i, slot(e, dy)], hub_recv.at[i, slot(e, dy)],
                    {"dp": dp_of(z - e + nz, y_at, core)},
                )

    ahead = 4
    for n in range(ahead):
        multiply(n)
    for n in range(len(schedule)):
        scatter(n)
        if n + ahead < len(schedule):
            multiply(n + ahead)

    for load in loads[3:]:
        load.wait()
    column[pl.ds(span, 8), :] = jnp.zeros((8, block), F32)
    fin = {}
    for i, h in enumerate(HUBS):
        own = schedule.index((h, h))
        value = leaf[own, y_hi].astype(F32)
        for e in [o - h for o in LEAVES[h]]:
            for dy in (0, 1):
                if e or dy:
                    to_hub[h, e, dy].wait()
                    value = value + hub_in[i, slot(e, dy)].astype(F32)
        column[pl.ds(0, span), :] = value
        for c in range(2):
            for k in range(2):
                cut = column[pl.ds(k * span // 2 + c * rows, pad), :]
                fin_out[i, c, pl.ds(k * pad, pad), :] = cut.astype(BF16)
        for dc in (1, 0):
            core_at = (core + dc) % 2
            if h or dc:
                fin[i, dc] = send(
                    fin_out.at[i, core_at], fin_in.at[i, dc],
                    fin_send.at[i, dc], fin_recv.at[i, dc],
                    {"dp": dp_of(z - h + nz, y_hi, core_at)},
                )

    for dc in range(2):
        for i, h in enumerate(HUBS):
            if h or dc:
                fin[i, dc].wait()
        for k in range(2):
            at = pl.ds(k * pad, pad)
            low_grad = (fin_in if dc else fin_out)[len(HUBS) - 1, 1 if dc else core, at, :].astype(F32)
            for i in range(len(HUBS) - 1):
                low_grad = low_grad + fin_in[i, dc, at, :].astype(F32)
            low_grad = low_grad[:rows]
            cut = pl.ds(pl.multiple_of(((core + dc) % 2) * 2 * block + k * block, block), block)
            moment_new = beta_one * first[:, cut] + (1.0 - beta_one) * low_grad
            second_new = beta_two * second[:, cut] + (1.0 - beta_two) * low_grad * low_grad
            direction = moment_new / corr_one / (jnp.sqrt(second_new / corr_two) + adam_eps)
            first_out[:, cut] = moment_new
            second_out[:, cut] = second_new
            padded = jnp.concatenate([direction, jnp.zeros((pad - rows, block), F32)], axis=0)
            dirs[0, :, cut] = padded.astype(BF16)

    gathered, returned = {}, {}
    for r in order:
        for dy in (1, 0):
            q = 2 * r + dy
            if q:
                gathered[q] = send(
                    dirs.at[0], dirs.at[q], dir_send.at[q], dir_recv.at[q], {"mp": mp_of(r, dy)},
                )
    for r in list(order[::-1]):
        for dy in range(2):
            if 2 * r + dy:
                gathered[2 * r + dy].wait()
        stacked = dirs[pl.ds(2 * r, 2)].reshape(2 * pad, rank)
        product = lax.dot_general(
            stacked, basis[...], (((1,), (1,)), ((), ())), preferred_element_type=F32
        ).astype(BF16)
        for dy in range(2):
            q = 2 * r + dy
            blocks[q] = product[dy * pad : (dy + 1) * pad]
            if q:
                returned[q] = send(
                    blocks.at[q], delta.at[q], blk_send.at[q], blk_recv.at[q], {"mp": mp_of(-r, dy)},
                )
    for r in list(order[::-1]):
        for dy in range(2):
            q = 2 * r + dy
            if q:
                returned[q].wait()
            at = pl.ds(pl.multiple_of(mp_of(r, dy) * width, width), width)
            change = (delta if q else blocks)[q].astype(F32)[:rows]
            weights_out[:, at] = (weights[:, at].astype(F32) - step_size * change).astype(BF16)


def on_device(nz, nx, acts, out_grads, basis, weights, first_moment, second_moment):
    tokens, width = acts.shape
    hidden = out_grads.shape[1]
    rank = basis.shape[1]
    rows, full = weights.shape
    pad = -(-rows // 16) * 16
    span = hidden // nz
    peers = 2 * nx
    piece = tokens // peers
    hubs = len(HUBS)
    dma = pltpu.SemaphoreType.DMA
    vmem = pltpu.VMEM
    return pl.pallas_call(
        functools.partial(kernel, nz, nx, pad),
        out_shape=(
            jax.ShapeDtypeStruct(weights.shape, BF16),
            jax.ShapeDtypeStruct(first_moment.shape, F32),
            jax.ShapeDtypeStruct(second_moment.shape, F32),
        ),
        in_specs=[pl.BlockSpec(memory_space=pl.ANY)] * 6,
        out_specs=[pl.BlockSpec(memory_space=pltpu.VMEM)] * 3,
        scratch_shapes=[
            vmem(acts.shape, BF16),
            vmem(out_grads.shape, BF16),
            vmem(basis.shape, BF16),
            vmem(weights.shape, BF16),
            vmem(first_moment.shape, F32),
            vmem(second_moment.shape, F32),
            vmem((tokens, rank), BF16),
            vmem((peers, piece, rank), BF16),
            vmem((tokens, rank), BF16),
            vmem((hidden, tokens), BF16),
            vmem((nz, 2, 2, span, rank // 4), BF16),
            vmem((nz, 2, span, rank // 4), BF16),
            vmem((nz, 2, span, rank // 4), BF16),
            vmem((hubs, 8, span, rank // 4), BF16),
            vmem((span + 8, rank // 4), F32),
            vmem((hubs, 2, 2 * pad, rank // 4), BF16),
            vmem((hubs, 2, 2 * pad, rank // 4), BF16),
            vmem((peers, pad, rank), BF16),
            vmem((peers, pad, width), BF16),
            vmem((peers, pad, width), BF16),
            dma((6,)),
            dma((peers,)), dma((peers,)), dma((peers,)), dma((peers,)),
            dma((nz,)), dma((nz,)),
            dma((hubs, 8)), dma((hubs, 8)), dma((hubs, 2)), dma((hubs, 2)),
            dma((peers,)), dma((peers,)), dma((peers,)), dma((peers,)),
        ],
        compiler_params=pltpu.CompilerParams(
            collective_id=0, has_side_effects=True, vmem_limit_bytes=60 * 1024 * 1024
        ),
    )(acts, out_grads, basis, weights, first_moment, second_moment)


def solution(mesh):
    nz, nx = mesh.shape["dp"] // 4, mesh.shape["mp"] // 2
    return jax.shard_map(
        functools.partial(on_device, nz, nx),
        mesh=mesh,
        in_specs=(
            P("dp", "mp"),
            P("dp", "mp"),
            P("mp", None),
            P(("mp", "dp"), None),
            P(("mp", "dp"), None),
            P(("mp", "dp"), None),
        ),
        out_specs=(P(("mp", "dp"), None), P(("mp", "dp"), None), P(("mp", "dp"), None)),
        check_vma=False,
    )
```

time: 87.6 us -> 75.3 us (0.86)
  Pallas kernels: 77.9 us -> 69.6 us
  local copies, waits for them, and re-layouts: 8.71 us -> 4.81 us
    pallas_call x1, Pallas kernels: 77.9 us -> 69.6 us  [on_device(): pl.pallas_call(functools.partial(kernel, nz, nx, pad), out_shape=(jax.Sha...]
    unnamed x15 -> x3, local copies, waits for them, and re-layouts: 8.71 us -> 4.81 us
where the time goes in v2:
time: 75.3 us; the launch traced here: 75.1 us
  Pallas kernels  69.6 us (92%)
  local copies, waits for them, and re-layouts  4.81 us (6%)
    pallas_call x1, Pallas kernels, on_device(): pl.pallas_call(functools.partial(kernel, nz, nx, pad), out_shape=(jax.Sha...  69.6 us
    unnamed x3, local copies, waits for them, and re-layouts  4.81 us

profile of v2, /device:TPU:1, one launch (start us, length us, event | category | flops | bytes accessed | tf_op | source)
XLA Modules:
  0.0 75.1 jit_solution(2331743928218403959)
XLA Ops:
  0.6 69.6 %shard_map.85 = (bf16[28,8192]{1,0:T(8,128)(2,1)}, f32[28,512]{1,0:T(8,128)}, f32[28,512]{1,0:T(8,128)}) custom-call(bf16[512,1024]{1,0:T(8,128)(2,1)} %acts_hbm.1, bf16[512,1792]{1,0:T(8,128)(2,1)} %grads_hbm.1, bf16[1024,512]{1,0:T(8,128)(2,1)} %basis_hbm.1, bf16[28,8192]{1,0:T(8,128)(2,1)} %weights_hbm.1, f32[28,512]{1,0:T(8,128)} %first_hbm.1, ...), custom_call_target="tpu_custom_call" | custom-call | tf_op jit(solution)/shard_map/pallas_call | solution.py:276
  70.2 1.9 %copy.12 = bf16[28,8192]{1,0:T(8,128)(2,1)} copy(bf16[28,8192]{1,0:T(8,128)(2,1)} %get-tuple-element.6) | data formatting | bytes 917504
  72.1 1.5 %copy.13 = f32[28,512]{1,0:T(8,128)} copy(f32[28,512]{1,0:T(8,128)} %get-tuple-element.7) | data formatting | bytes 114688
  73.6 1.5 %copy.14 = f32[28,512]{1,0:T(8,128)} copy(f32[28,512]{1,0:T(8,128)} %get-tuple-element.8) | data formatting | bytes 114688

commit v3 on v2

v3 whole, which is shorter than its diff:
```python
import functools

import jax
import jax.numpy as jnp
from jax import lax
from jax.experimental import pallas as pl
from jax.experimental.pallas import tpu as pltpu
from jax.sharding import PartitionSpec as P

beta_one = 0.9
beta_two = 0.99
corr_one = 1.0 - 0.9**10
corr_two = 1.0 - 0.99**10
adam_eps = 1e-08
step_size = 1.0

HUBS = (6, -6, 3, -3, 0)
LEAVES = {6: (8, 7, 5, 6), -6: (-7, -5, -6), 3: (4, 2, 3), -3: (-4, -2, -3), 0: (1, -1, 0)}

MESH = pl.DeviceIdType.MESH
F32 = jnp.float32
BF16 = jnp.bfloat16


def kernel(
    nz, nx, pad,
    acts_hbm, grads_hbm, basis_hbm, weights_hbm, first_hbm, second_hbm,
    weights_out, first_out, second_out,
    acts, grads, basis, weights, first, second,
    part, part_in, proj, turned,
    halves, sibling_in, leaf, hub_in, column, fin_out, fin_in, dirs, blocks, delta,
    load_sem, rs_send, rs_recv, ag_send, ag_recv, core_send, core_recv,
    hub_send, hub_recv, fin_send, fin_recv,
    dir_send, dir_recv, blk_send, blk_recv, relay_sem,
):
    dp, mp = lax.axis_index("dp"), lax.axis_index("mp")
    z, y_hi, core = dp // 4, (dp // 2) % 2, dp % 2
    x, y_lo = mp // 2, mp % 2
    tokens, width = acts.shape
    hidden = turned.shape[0]
    rank = basis.shape[1]
    rows = first.shape[0]
    span = hidden // nz
    piece = tokens // (2 * nx)

    def dp_of(z_at, y_at, core_at):
        return (z_at % nz) * 4 + y_at * 2 + core_at

    def mp_of(r, dy):
        return ((x + r + nx) % nx) * 2 + (y_lo + dy) % 2

    loads = [
        pltpu.make_async_copy(src, dst, load_sem.at[i])
        for i, (src, dst) in enumerate(
            (
                (basis_hbm, basis),
                (acts_hbm, acts),
                (grads_hbm, grads),
                (weights_hbm, weights),
                (first_hbm, first),
                (second_hbm, second),
            )
        )
    ]
    for load in loads:
        load.start()

    relations = [(r, dy) for r in range(nx) for dy in range(2)]
    peers = [({"mp": mp_of(r, dy)}) for r, dy in relations[1:]]
    peers += [
        {"dp": dp_of(z, y_hi, 1 - core)},
        {"dp": dp_of(z, 1 - y_hi, core)},
        {"dp": dp_of(z + 1, y_hi, core)},
        {"dp": dp_of(z + nz - 1, y_hi, core)},
    ]
    barrier = pltpu.get_barrier_semaphore()
    for peer in peers:
        pl.semaphore_signal(barrier, inc=1, device_id=peer, device_id_type=MESH)

    def tell(n):
        for i, dz in enumerate((n, -n)):
            pl.semaphore_signal(
                relay_sem.at[n - 1, i], inc=1,
                device_id={"dp": dp_of(z + dz + nz, y_hi, core)}, device_id_type=MESH,
            )

    def hear(n):
        for i in range(2):
            pl.semaphore_wait(relay_sem.at[n - 1, i], 1)

    def send(src, dst, send_sem, recv_sem, device):
        copy = pltpu.make_async_remote_copy(
            src_ref=src, dst_ref=dst, send_sem=send_sem, recv_sem=recv_sem,
            device_id=device, device_id_type=MESH,
        )
        copy.start()
        return copy

    loads[0].wait()
    loads[1].wait()

    half = rank // 2

    def project(s, r):
        at = pl.ds(pl.multiple_of(((x + r) % nx) * 2 * piece, 2 * piece), 2 * piece)
        value = jnp.dot(
            acts[at, :], basis[:, s * half : (s + 1) * half], preferred_element_type=F32
        )
        part[s, at, :] = value.astype(BF16)

    def piece_of(index):
        return pl.ds(pl.multiple_of(index * piece, piece), piece)

    order = [nx // 2] * (nx > 1) + [r for r in range(1, nx) if r != nx // 2] + [0]
    rs = {}
    for s in range(2):
        for r in order:
            project(s, r)
            if s == 0 and r == order[0]:
                pl.semaphore_wait(barrier, len(peers))
                tell(1)
            for dy in (1, 0):
                q = 2 * r + dy
                if q:
                    rs[s, q] = send(
                        part.at[s, piece_of(mp_of(r, dy)), :], part_in.at[s, q],
                        rs_send.at[s, q], rs_recv.at[s, q], {"mp": mp_of(r, dy)},
                    )

    loads[2].wait()
    for b in range(hidden // 128):
        turned[pl.ds(b * 128, 128), :] = grads[:, pl.ds(b * 128, 128)].T
    hear(1)
    tell(2)

    ag = {}
    for s in range(2):
        total = part[s, piece_of(mp), :].astype(F32)
        for q in range(1, 2 * nx):
            rs[s, q].wait()
            total = total + part_in[s, q].astype(F32)
        proj[s, piece_of(mp), :] = total.astype(BF16)
        for r in order:
            for dy in (1, 0):
                q = 2 * r + dy
                if q:
                    ag[s, q] = send(
                        proj.at[s, piece_of(mp), :], proj.at[s, piece_of(mp), :],
                        ag_send.at[s, q], ag_recv.at[s, q], {"mp": mp_of(r, dy)},
                    )
    hear(2)
    tell(3)

    schedule = [(h, o) for h in HUBS for o in LEAVES[h]]
    block = rank // 4
    siblings, to_hub = {}, {}

    def multiply(s, n):
        at = (z - schedule[n][1] + nz) % nz
        value = jnp.dot(
            turned[pl.ds(pl.multiple_of(at * span, 16), span), :], proj[s],
            preferred_element_type=F32,
        ).reshape(2, span // 2, half)
        for c in range(2):
            halves[s, n, c] = value[:, :, c * block : (c + 1) * block].astype(BF16)
        siblings[s, n] = send(
            halves.at[s, n, 1 - core], sibling_in.at[s, n],
            core_send.at[s, n], core_recv.at[s, n], {"dp": dp_of(z, y_hi, 1 - core)},
        )

    def slot(e, dy):
        return (e + 1) * 2 + dy

    def scatter(s, n):
        h, o = schedule[n]
        e = o - h
        i = HUBS.index(h)
        siblings[s, n].wait()
        value = halves[s, n, core].astype(F32) + sibling_in[s, n].astype(F32)
        leaf[s, n] = value.astype(BF16)
        for dy in (1, 0):
            if e or dy:
                y_at = (y_hi + dy) % 2
                to_hub[s, h, e, dy] = send(
                    leaf.at[s, n, y_at], hub_in.at[s, i, slot(e, dy)],
                    hub_send.at[s, i, slot(e, dy)], hub_recv.at[s, i, slot(e, dy)],
                    {"dp": dp_of(z - e + nz, y_at, core)},
                )

    ahead = 4
    for s in range(2):
        for q in range(1, 2 * nx):
            ag[s, q].wait()
        for n in range(ahead):
            multiply(s, n)
        for n in range(len(schedule)):
            scatter(s, n)
            if n + ahead < len(schedule):
                multiply(s, n + ahead)
    hear(3)

    for load in loads[3:]:
        load.wait()
    column[:, pl.ds(span // 2, 8), :] = jnp.zeros((2, 8, block), F32)
    fin = {}
    for i, h in enumerate(HUBS):
        own = schedule.index((h, h))
        for s in range(2):
            value = leaf[s, own, y_hi].astype(F32)
            for e in [o - h for o in LEAVES[h]]:
                for dy in (0, 1):
                    if e or dy:
                        to_hub[s, h, e, dy].wait()
                        value = value + hub_in[s, i, slot(e, dy)].astype(F32)
            column[s, pl.ds(0, span // 2), :] = value
            for c in range(2):
                cut = column[s, pl.ds(c * rows, pad), :]
                fin_out[i, c, pl.ds(s * pad, pad), :] = cut.astype(BF16)
        for dc in (1, 0):
            core_at = (core + dc) % 2
            if h or dc:
                fin[i, dc] = send(
                    fin_out.at[i, core_at], fin_in.at[i, dc],
                    fin_send.at[i, dc], fin_recv.at[i, dc],
                    {"dp": dp_of(z - h + nz, y_hi, core_at)},
                )

    for dc in range(2):
        for i, h in enumerate(HUBS):
            if h or dc:
                fin[i, dc].wait()
        for k in range(2):
            at = pl.ds(k * pad, pad)
            low_grad = (fin_in if dc else fin_out)[len(HUBS) - 1, 1 if dc else core, at, :].astype(F32)
            for i in range(len(HUBS) - 1):
                low_grad = low_grad + fin_in[i, dc, at, :].astype(F32)
            low_grad = low_grad[:rows]
            cut = pl.ds(pl.multiple_of((2 * k + (core + dc) % 2) * block, block), block)
            moment_new = beta_one * first[:, cut] + (1.0 - beta_one) * low_grad
            second_new = beta_two * second[:, cut] + (1.0 - beta_two) * low_grad * low_grad
            direction = moment_new / corr_one / (jnp.sqrt(second_new / corr_two) + adam_eps)
            first_out[:, cut] = moment_new
            second_out[:, cut] = second_new
            padded = jnp.concatenate([direction, jnp.zeros((pad - rows, block), F32)], axis=0)
            dirs[0, :, cut] = padded.astype(BF16)

    gathered, returned = {}, {}
    for r in order:
        for dy in (1, 0):
            q = 2 * r + dy
            if q:
                gathered[q] = send(
                    dirs.at[0], dirs.at[q], dir_send.at[q], dir_recv.at[q], {"mp": mp_of(r, dy)},
                )
    for r in list(order[::-1]):
        for dy in range(2):
            if 2 * r + dy:
                gathered[2 * r + dy].wait()
        stacked = dirs[pl.ds(2 * r, 2)].reshape(2 * pad, rank)
        product = lax.dot_general(
            stacked, basis[...], (((1,), (1,)), ((), ())), preferred_element_type=F32
        ).astype(BF16)
        for dy in range(2):
            q = 2 * r + dy
            blocks[q] = product[dy * pad : (dy + 1) * pad]
            if q:
                returned[q] = send(
                    blocks.at[q], delta.at[q], blk_send.at[q], blk_recv.at[q], {"mp": mp_of(-r, dy)},
                )
    for r in list(order[::-1]):
        for dy in range(2):
            q = 2 * r + dy
            if q:
                returned[q].wait()
            at = pl.ds(pl.multiple_of(mp_of(r, dy) * width, width), width)
            change = (delta if q else blocks)[q].astype(F32)[:rows]
            weights_out[:, at] = (weights[:, at].astype(F32) - step_size * change).astype(BF16)


def hand_over(*refs):
    copies = [pltpu.make_async_copy(refs[i], refs[3 + i], refs[6].at[i]) for i in range(3)]
    for copy in copies:
        copy.start()
    for copy in copies:
        copy.wait()


def on_device(nz, nx, acts, out_grads, basis, weights, first_moment, second_moment):
    tokens, width = acts.shape
    hidden = out_grads.shape[1]
    rank = basis.shape[1]
    rows, full = weights.shape
    pad = -(-rows // 16) * 16
    span = hidden // nz
    peers = 2 * nx
    piece = tokens // peers
    hubs = len(HUBS)
    arrays = (acts, out_grads, basis, weights, first_moment, second_moment)
    held = [pltpu.with_memory_space_constraint(array, pltpu.HBM) for array in arrays]
    dma = pltpu.SemaphoreType.DMA
    vmem = pltpu.VMEM
    results = pl.pallas_call(
        functools.partial(kernel, nz, nx, pad),
        out_shape=(
            jax.ShapeDtypeStruct(weights.shape, BF16),
            jax.ShapeDtypeStruct(first_moment.shape, F32),
            jax.ShapeDtypeStruct(second_moment.shape, F32),
        ),
        in_specs=[pl.BlockSpec(memory_space=pltpu.HBM)] * 6,
        out_specs=[pl.BlockSpec(memory_space=pltpu.VMEM)] * 3,
        scratch_shapes=[
            vmem(acts.shape, BF16),
            vmem(out_grads.shape, BF16),
            vmem(basis.shape, BF16),
            vmem(weights.shape, BF16),
            vmem(first_moment.shape, F32),
            vmem(second_moment.shape, F32),
            vmem((2, tokens, rank // 2), BF16),
            vmem((2, peers, piece, rank // 2), BF16),
            vmem((2, tokens, rank // 2), BF16),
            vmem((hidden, tokens), BF16),
            vmem((2, nz, 2, 2, span // 2, rank // 4), BF16),
            vmem((2, nz, 2, span // 2, rank // 4), BF16),
            vmem((2, nz, 2, span // 2, rank // 4), BF16),
            vmem((2, hubs, 8, span // 2, rank // 4), BF16),
            vmem((2, span // 2 + 8, rank // 4), F32),
            vmem((hubs, 2, 2 * pad, rank // 4), BF16),
            vmem((hubs, 2, 2 * pad, rank // 4), BF16),
            vmem((peers, pad, rank), BF16),
            vmem((peers, pad, width), BF16),
            vmem((peers, pad, width), BF16),
            dma((6,)),
            dma((2, peers)), dma((2, peers)), dma((2, peers)), dma((2, peers)),
            dma((2, nz)), dma((2, nz)),
            dma((2, hubs, 8)), dma((2, hubs, 8)), dma((hubs, 2)), dma((hubs, 2)),
            dma((peers,)), dma((peers,)), dma((peers,)), dma((peers,)),
            pltpu.SemaphoreType.REGULAR((3, 2)),
        ],
        compiler_params=pltpu.CompilerParams(
            collective_id=0, has_side_effects=True, vmem_limit_bytes=32 * 1024 * 1024
        ),
    )(*held)
    return pl.pallas_call(
        hand_over,
        out_shape=tuple(jax.ShapeDtypeStruct(r.shape, r.dtype) for r in results),
        in_specs=[pl.BlockSpec(memory_space=pl.ANY)] * 3,
        out_specs=[pl.BlockSpec(memory_space=pltpu.HBM)] * 3,
        scratch_shapes=[dma((3,))],
    )(*results)


def solution(mesh):
    nz, nx = mesh.shape["dp"] // 4, mesh.shape["mp"] // 2
    return jax.shard_map(
        functools.partial(on_device, nz, nx),
        mesh=mesh,
        in_specs=(
            P("dp", "mp"),
            P("dp", "mp"),
            P("mp", None),
            P(("mp", "dp"), None),
            P(("mp", "dp"), None),
            P(("mp", "dp"), None),
        ),
        out_specs=(P(("mp", "dp"), None), P(("mp", "dp"), None), P(("mp", "dp"), None)),
        check_vma=False,
    )
```

time: 75.3 us -> 89 us (1.18)
  the two profiles are of different devices: /device:TPU:1 before, /device:TPU:64 now
where the time goes in v3:
time: 89 us; the launch traced here: 88.9 us
  Pallas kernels  86.2 us (97%)
  local copies, waits for them, and re-layouts  2.02 us (2%)
    pallas_call x1, Pallas kernels, on_device(): pl.pallas_call(functools.partial(kernel, nz, nx, pad), out_shape=(jax.Sha...  65.2 us
    pallas_call x1, Pallas kernels, on_device(): pl.pallas_call(hand_over, out_shape=tuple((jax.ShapeDtypeStruct(r.shape,...  21 us
    unnamed x6, local copies, waits for them, and re-layouts  2.02 us

profile of v3, /device:TPU:64, one launch (start us, length us, event | category | flops | bytes accessed | tf_op | source)
XLA Modules:
  0.0 88.9 jit_solution(13734906614697085127)
XLA Ops:
  0.6 65.2 %shard_map.85 = (bf16[28,8192]{1,0:T(8,128)(2,1)S(1)}, f32[28,512]{1,0:T(8,128)S(1)}, f32[28,512]{1,0:T(8,128)S(1)}) custom-call(bf16[512,1024]{1,0:T(8,128)(2,1)} %acts_hbm.1, bf16[512,1792]{1,0:T(8,128)(2,1)} %grads_hbm.1, bf16[1024,512]{1,0:T(8,128)(2,1)} %basis_hbm.1, bf16[28,8192]{1,0:T(8,128)(2,1)} %weights_hbm.1, f32[28,512]{1,0:T(8,128)} %first_hbm.1, ...), custom_call_target="tpu_custom_call" | custom-call | tf_op jit(solution)/shard_map/pallas_call | solution.py:302
  65.9 0.0 copy-start
  65.9 0.8 copy-done
  66.7 0.0 copy-start.1
  66.7 0.6 copy-done.1
  67.3 0.0 copy-start.2
  67.3 0.6 copy-done.2
  67.9 21.0 %shard_map.86 = (bf16[28,8192]{1,0:T(8,128)(2,1)}, f32[28,512]{1,0:T(8,128)}, f32[28,512]{1,0:T(8,128)}) custom-call(bf16[28,8192]{1,0:T(8,128)(2,1)} %copy-done, f32[28,512]{1,0:T(8,128)} %copy-done.1, f32[28,512]{1,0:T(8,128)} %copy-done.2), custom_call_target="tpu_custom_call" | custom-call | tf_op jit(solution)/shard_map/pallas_call | solution.py:343
Async XLA Ops:
  65.9 0.8 copy-start
  66.7 0.6 copy-start.1
  67.3 0.6 copy-start.2

commit v4 on v3

--- a/solution.py
+++ b/solution.py
@@ -62,7 +62,7 @@
             )
         )
     ]
-    for load in loads:
+    for load in loads[:2]:
         load.start()
 
     relations = [(r, dy) for r in range(nx) for dy in range(2)]
@@ -98,15 +98,10 @@
 
     loads[0].wait()
     loads[1].wait()
+    for load in loads[2:]:
+        load.start()
 
     half = rank // 2
-
-    def project(s, r):
-        at = pl.ds(pl.multiple_of(((x + r) % nx) * 2 * piece, 2 * piece), 2 * piece)
-        value = jnp.dot(
-            acts[at, :], basis[:, s * half : (s + 1) * half], preferred_element_type=F32
-        )
-        part[s, at, :] = value.astype(BF16)
 
     def piece_of(index):
         return pl.ds(pl.multiple_of(index * piece, piece), piece)
@@ -114,11 +109,14 @@
     order = [nx // 2] * (nx > 1) + [r for r in range(1, nx) if r != nx // 2] + [0]
     rs = {}
     for s in range(2):
+        value = jnp.dot(
+            acts[...], basis[:, s * half : (s + 1) * half], preferred_element_type=F32
+        )
+        part[s] = value.astype(BF16)
+        if s == 0:
+            pl.semaphore_wait(barrier, len(peers))
+            tell(1)
         for r in order:
-            project(s, r)
-            if s == 0 and r == order[0]:
-                pl.semaphore_wait(barrier, len(peers))
-                tell(1)
             for dy in (1, 0):
                 q = 2 * r + dy
                 if q:
@@ -155,48 +153,54 @@
     block = rank // 4
     siblings, to_hub = {}, {}
 
-    def multiply(s, n):
-        at = (z - schedule[n][1] + nz) % nz
-        value = jnp.dot(
-            turned[pl.ds(pl.multiple_of(at * span, 16), span), :], proj[s],
-            preferred_element_type=F32,
-        ).reshape(2, span // 2, half)
-        for c in range(2):
-            halves[s, n, c] = value[:, :, c * block : (c + 1) * block].astype(BF16)
-        siblings[s, n] = send(
-            halves.at[s, n, 1 - core], sibling_in.at[s, n],
-            core_send.at[s, n], core_recv.at[s, n], {"dp": dp_of(z, y_hi, 1 - core)},
-        )
+    group = 4
+
+    def multiply(s):
+        for b in range(nz // group):
+            value = jnp.dot(
+                turned[pl.ds(b * group * span, group * span), :], proj[s],
+                preferred_element_type=F32,
+            ).reshape(group, 2, span // 2, half)
+            for c in range(2):
+                halves[s, c, pl.ds(b * group, group)] = value[
+                    :, :, :, c * block : (c + 1) * block
+                ].astype(BF16)
+        for n, (h, o) in enumerate(schedule):
+            at = (z - o + nz) % nz
+            siblings[s, n] = send(
+                halves.at[s, 1 - core, at], sibling_in.at[s, n],
+                core_send.at[s, n], core_recv.at[s, n], {"dp": dp_of(z, y_hi, 1 - core)},
+            )
 
     def slot(e, dy):
         return (e + 1) * 2 + dy
 
-    def scatter(s, n):
-        h, o = schedule[n]
-        e = o - h
+    def scatter(s, h):
         i = HUBS.index(h)
-        siblings[s, n].wait()
-        value = halves[s, n, core].astype(F32) + sibling_in[s, n].astype(F32)
-        leaf[s, n] = value.astype(BF16)
-        for dy in (1, 0):
-            if e or dy:
-                y_at = (y_hi + dy) % 2
-                to_hub[s, h, e, dy] = send(
-                    leaf.at[s, n, y_at], hub_in.at[s, i, slot(e, dy)],
-                    hub_send.at[s, i, slot(e, dy)], hub_recv.at[s, i, slot(e, dy)],
-                    {"dp": dp_of(z - e + nz, y_at, core)},
-                )
-
-    ahead = 4
+        members = [n for n in range(nz) if schedule[n][0] == h]
+        for n in members:
+            siblings[s, n].wait()
+        for n in members:
+            at = (z - schedule[n][1] + nz) % nz
+            value = halves[s, core, at].astype(F32) + sibling_in[s, n].astype(F32)
+            leaf[s, n] = value.astype(BF16)
+        for n in members:
+            e = schedule[n][1] - h
+            for dy in (1, 0):
+                if e or dy:
+                    y_at = (y_hi + dy) % 2
+                    to_hub[s, h, e, dy] = send(
+                        leaf.at[s, n, y_at], hub_in.at[s, i, slot(e, dy)],
+                        hub_send.at[s, i, slot(e, dy)], hub_recv.at[s, i, slot(e, dy)],
+                        {"dp": dp_of(z - e + nz, y_at, core)},
+                    )
+
     for s in range(2):
         for q in range(1, 2 * nx):
             ag[s, q].wait()
-        for n in range(ahead):
-            multiply(s, n)
-        for n in range(len(schedule)):
-            scatter(s, n)
-            if n + ahead < len(schedule):
-                multiply(s, n + ahead)
+        multiply(s)
+        for h in HUBS:
+            scatter(s, h)
     hear(3)
 
     for load in loads[3:]:
@@ -277,14 +281,6 @@
             weights_out[:, at] = (weights[:, at].astype(F32) - step_size * change).astype(BF16)
 
 
-def hand_over(*refs):
-    copies = [pltpu.make_async_copy(refs[i], refs[3 + i], refs[6].at[i]) for i in range(3)]
-    for copy in copies:
-        copy.start()
-    for copy in copies:
-        copy.wait()
-
-
 def on_device(nz, nx, acts, out_grads, basis, weights, first_moment, second_moment):
     tokens, width = acts.shape
     hidden = out_grads.shape[1]
@@ -299,7 +295,7 @@
     held = [pltpu.with_memory_space_constraint(array, pltpu.HBM) for array in arrays]
     dma = pltpu.SemaphoreType.DMA
     vmem = pltpu.VMEM
-    results = pl.pallas_call(
+    return pl.pallas_call(
         functools.partial(kernel, nz, nx, pad),
         out_shape=(
             jax.ShapeDtypeStruct(weights.shape, BF16),
@@ -319,7 +315,7 @@
             vmem((2, peers, piece, rank // 2), BF16),
             vmem((2, tokens, rank // 2), BF16),
             vmem((hidden, tokens), BF16),
-            vmem((2, nz, 2, 2, span // 2, rank // 4), BF16),
+            vmem((2, 2, nz, 2, span // 2, rank // 4), BF16),
             vmem((2, nz, 2, span // 2, rank // 4), BF16),
             vmem((2, nz, 2, span // 2, rank // 4), BF16),
             vmem((2, hubs, 8, span // 2, rank // 4), BF16),
@@ -340,13 +336,6 @@
             collective_id=0, has_side_effects=True, vmem_limit_bytes=32 * 1024 * 1024
         ),
     )(*held)
-    return pl.pallas_call(
-        hand_over,
-        out_shape=tuple(jax.ShapeDtypeStruct(r.shape, r.dtype) for r in results),
-        in_specs=[pl.BlockSpec(memory_space=pl.ANY)] * 3,
-        out_specs=[pl.BlockSpec(memory_space=pltpu.HBM)] * 3,
-        scratch_shapes=[dma((3,))],
-    )(*results)
 
 
 def solution(mesh):

time: 89 us -> 68.4 us (0.77)
  the two profiles are of different devices: /device:TPU:64 before, /device:TPU:32 now
where the time goes in v4:
time: 68.4 us; the launch traced here: 68.2 us
  Pallas kernels  65.5 us (96%)
  local copies, waits for them, and re-layouts  2.05 us (3%)
    pallas_call x1, Pallas kernels, on_device(): pl.pallas_call(functools.partial(kernel, nz, nx, pad), out_shape=(jax.Sha...  65.5 us
    unnamed x3, local copies, waits for them, and re-layouts  2.05 us

profile of v4, /device:TPU:32, one launch (start us, length us, event | category | flops | bytes accessed | tf_op | source)
XLA Modules:
  0.0 68.2 jit_solution(11245619764422671596)
XLA Ops:
  0.6 65.5 %shard_map.85 = (bf16[28,8192]{1,0:T(8,128)(2,1)S(1)}, f32[28,512]{1,0:T(8,128)S(1)}, f32[28,512]{1,0:T(8,128)S(1)}) custom-call(bf16[512,1024]{1,0:T(8,128)(2,1)} %acts_hbm.1, bf16[512,1792]{1,0:T(8,128)(2,1)} %grads_hbm.1, bf16[1024,512]{1,0:T(8,128)(2,1)} %basis_hbm.1, bf16[28,8192]{1,0:T(8,128)(2,1)} %weights_hbm.1, f32[28,512]{1,0:T(8,128)} %first_hbm.1, ...), custom_call_target="tpu_custom_call" | custom-call | tf_op jit(solution)/shard_map/pallas_call | solution.py:298
  66.1 0.8 %copy.12 = bf16[28,8192]{1,0:T(8,128)(2,1)} copy(bf16[28,8192]{1,0:T(8,128)(2,1)S(1)} %get-tuple-element.6) | data formatting | bytes 917504
  66.9 0.6 copy.13
  67.6 0.6 copy.14

commit v5 on v4

--- a/solution.py
+++ b/solution.py
@@ -15,6 +15,7 @@
 step_size = 1.0
 
 HUBS = (6, -6, 3, -3, 0)
+HELPERS = ((0, "row"), (1, "row"), (-1, "row"), (0, "inner"), (0, "outer"), (1, "inner"), (-1, "outer"))
 LEAVES = {6: (8, 7, 5, 6), -6: (-7, -5, -6), 3: (4, 2, 3), -3: (-4, -2, -3), 0: (1, -1, 0)}
 
 MESH = pl.DeviceIdType.MESH
@@ -22,16 +23,22 @@
 BF16 = jnp.bfloat16
 
 
+def moments(first, second, low_grad):
+    moment_new = beta_one * first + (1.0 - beta_one) * low_grad
+    second_new = beta_two * second + (1.0 - beta_two) * low_grad * low_grad
+    return moment_new, second_new
+
+
 def kernel(
     nz, nx, pad,
     acts_hbm, grads_hbm, basis_hbm, weights_hbm, first_hbm, second_hbm,
-    weights_out, first_out, second_out,
+    weights_out, grad_out,
     acts, grads, basis, weights, first, second,
     part, part_in, proj, turned,
     halves, sibling_in, leaf, hub_in, column, fin_out, fin_in, dirs, blocks, delta,
     load_sem, rs_send, rs_recv, ag_send, ag_recv, core_send, core_recv,
     hub_send, hub_recv, fin_send, fin_recv,
-    dir_send, dir_recv, blk_send, blk_recv, relay_sem,
+    dir_send, dir_recv, blk_send, blk_recv, relay_sem, far_basis, far_send, far_recv,
 ):
     dp, mp = lax.axis_index("dp"), lax.axis_index("mp")
     z, y_hi, core = dp // 4, (dp // 2) % 2, dp % 2
@@ -48,6 +55,10 @@
 
     def mp_of(r, dy):
         return ((x + r + nx) % nx) * 2 + (y_lo + dy) % 2
+
+    def device_of(r, via):
+        y_at = 1 - y_hi if via == "outer" else y_hi
+        return {"dp": dp_of(z, y_at, core), "mp": mp_of(r, 0 if via == "row" else 1)}
 
     loads = [
         pltpu.make_async_copy(src, dst, load_sem.at[i])
@@ -73,6 +84,7 @@
         {"dp": dp_of(z + 1, y_hi, core)},
         {"dp": dp_of(z + nz - 1, y_hi, core)},
     ]
+    peers += [device_of(r, "outer") for r in (-1, 0, 1)]
     barrier = pltpu.get_barrier_semaphore()
     for peer in peers:
         pl.semaphore_signal(barrier, inc=1, device_id=peer, device_id_type=MESH)
@@ -198,6 +210,12 @@
     for s in range(2):
         for q in range(1, 2 * nx):
             ag[s, q].wait()
+        if s == 1:
+            mine = pl.ds(pl.multiple_of(core * (width // 2), width // 2), width // 2)
+            far = send(
+                basis.at[mine, :], far_basis.at[mine, :], far_send.at[0], far_recv.at[0],
+                device_of(2, "row"),
+            )
         multiply(s)
         for h in HUBS:
             scatter(s, h)
@@ -229,6 +247,11 @@
                     {"dp": dp_of(z - h + nz, y_hi, core_at)},
                 )
 
+    far.wait()
+    swap = send(
+        far_basis.at[mine, :], far_basis.at[mine, :], far_send.at[1], far_recv.at[1],
+        {"dp": dp_of(z, y_hi, 1 - core)},
+    )
     for dc in range(2):
         for i, h in enumerate(HUBS):
             if h or dc:
@@ -240,45 +263,52 @@
                 low_grad = low_grad + fin_in[i, dc, at, :].astype(F32)
             low_grad = low_grad[:rows]
             cut = pl.ds(pl.multiple_of((2 * k + (core + dc) % 2) * block, block), block)
-            moment_new = beta_one * first[:, cut] + (1.0 - beta_one) * low_grad
-            second_new = beta_two * second[:, cut] + (1.0 - beta_two) * low_grad * low_grad
+            moment_new, second_new = moments(first[:, cut], second[:, cut], low_grad)
             direction = moment_new / corr_one / (jnp.sqrt(second_new / corr_two) + adam_eps)
-            first_out[:, cut] = moment_new
-            second_out[:, cut] = second_new
+            grad_out[:, cut] = low_grad
             padded = jnp.concatenate([direction, jnp.zeros((pad - rows, block), F32)], axis=0)
             dirs[0, :, cut] = padded.astype(BF16)
 
     gathered, returned = {}, {}
-    for r in order:
-        for dy in (1, 0):
-            q = 2 * r + dy
-            if q:
-                gathered[q] = send(
-                    dirs.at[0], dirs.at[q], dir_send.at[q], dir_recv.at[q], {"mp": mp_of(r, dy)},
-                )
-    for r in list(order[::-1]):
-        for dy in range(2):
-            if 2 * r + dy:
-                gathered[2 * r + dy].wait()
-        stacked = dirs[pl.ds(2 * r, 2)].reshape(2 * pad, rank)
+    for k in (5, 6, 4, 3, 1, 2):
+        gathered[k] = send(
+            dirs.at[0], dirs.at[k], dir_send.at[k], dir_recv.at[k], device_of(*HELPERS[k]),
+        )
+
+    def update(slots, shard):
+        stacked = jnp.concatenate([dirs[k] for k in slots], axis=0)
         product = lax.dot_general(
-            stacked, basis[...], (((1,), (1,)), ((), ())), preferred_element_type=F32
+            stacked, shard[...], (((1,), (1,)), ((), ())), preferred_element_type=F32
         ).astype(BF16)
-        for dy in range(2):
-            q = 2 * r + dy
-            blocks[q] = product[dy * pad : (dy + 1) * pad]
-            if q:
-                returned[q] = send(
-                    blocks.at[q], delta.at[q], blk_send.at[q], blk_recv.at[q], {"mp": mp_of(-r, dy)},
-                )
-    for r in list(order[::-1]):
-        for dy in range(2):
-            q = 2 * r + dy
-            if q:
-                returned[q].wait()
-            at = pl.ds(pl.multiple_of(mp_of(r, dy) * width, width), width)
-            change = (delta if q else blocks)[q].astype(F32)[:rows]
-            weights_out[:, at] = (weights[:, at].astype(F32) - step_size * change).astype(BF16)
+        return [product[i * pad : (i + 1) * pad] for i in range(len(slots))]
+
+    def give_back(k, value):
+        r, via = HELPERS[k]
+        blocks[k] = value
+        returned[k] = send(
+            blocks.at[k], delta.at[k], blk_send.at[k], blk_recv.at[k], device_of(-r, via),
+        )
+
+    def apply(r, via, change):
+        at = pl.ds(pl.multiple_of(mp_of(r, 0 if via == "row" else 1) * width, width), width)
+        change = change.astype(F32)[:rows]
+        weights_out[:, at] = (weights[:, at].astype(F32) - step_size * change).astype(BF16)
+
+    near = (5, 6, 3, 1, 2)
+    for k in near:
+        gathered[k].wait()
+    for k, value in zip(near, update(near, basis)):
+        give_back(k, value)
+    swap.wait()
+    gathered[4].wait()
+    value, own = update((4, 0), far_basis)
+    give_back(4, value)
+    apply(2, "row", own)
+    apply(0, "row", update((0,), basis)[0])
+    for k in (3, 1, 2, 4, 5, 6):
+        returned[k].wait()
+        r, via = HELPERS[k]
+        apply(r + 2 if k == 4 else r, via, delta[k])
 
 
 def on_device(nz, nx, acts, out_grads, basis, weights, first_moment, second_moment):
@@ -295,15 +325,14 @@
     held = [pltpu.with_memory_space_constraint(array, pltpu.HBM) for array in arrays]
     dma = pltpu.SemaphoreType.DMA
     vmem = pltpu.VMEM
-    return pl.pallas_call(
+    new_weights, low_grad = pl.pallas_call(
         functools.partial(kernel, nz, nx, pad),
         out_shape=(
             jax.ShapeDtypeStruct(weights.shape, BF16),
             jax.ShapeDtypeStruct(first_moment.shape, F32),
-            jax.ShapeDtypeStruct(second_moment.shape, F32),
         ),
         in_specs=[pl.BlockSpec(memory_space=pltpu.HBM)] * 6,
-        out_specs=[pl.BlockSpec(memory_space=pltpu.VMEM)] * 3,
+        out_specs=[pl.BlockSpec(memory_space=pltpu.VMEM)] * 2,
         scratch_shapes=[
             vmem(acts.shape, BF16),
             vmem(out_grads.shape, BF16),
@@ -331,11 +360,15 @@
             dma((2, hubs, 8)), dma((2, hubs, 8)), dma((hubs, 2)), dma((hubs, 2)),
             dma((peers,)), dma((peers,)), dma((peers,)), dma((peers,)),
             pltpu.SemaphoreType.REGULAR((3, 2)),
+            vmem(basis.shape, BF16),
+            dma((2,)), dma((2,)),
         ],
         compiler_params=pltpu.CompilerParams(
             collective_id=0, has_side_effects=True, vmem_limit_bytes=32 * 1024 * 1024
         ),
     )(*held)
+    moment_new, second_new = moments(first_moment, second_moment, low_grad)
+    return new_weights, moment_new, second_new
 
 
 def solution(mesh):

time: 68.4 us -> 65.4 us (0.956)
  Pallas kernels: 65.5 us -> 63.1 us
  local copies, waits for them, and re-layouts: 2.05 us -> 0.8 us
    pallas_call x1, Pallas kernels: 65.5 us -> 63.1 us  [on_device(): pl.pallas_call(functools.partial(kernel, nz, nx, pad), out_shape=(jax.Sha...]
    unnamed x3 -> x5, local copies, waits for them, and re-layouts: 2.05 us -> 0.8 us
where the time goes in v5:
time: 65.4 us; the launch traced here: 65.3 us
  Pallas kernels  63.1 us (96%)
  local copies, waits for them, and re-layouts  0.8 us (1%)
  other arithmetic  0.67 us (1%)
  between operations  0.67 us (1%)
    pallas_call x1, Pallas kernels, on_device(): pl.pallas_call(functools.partial(kernel, nz, nx, pad), out_shape=(jax.Sha...  63.1 us

profile of v5, /device:TPU:32, one launch (start us, length us, event | category | flops | bytes accessed | tf_op | source)
XLA Modules:
  0.0 65.3 jit_solution(8667685444133025975)
XLA Ops:
  0.6 0.0 copy-start.1
  0.6 0.0 copy-start
  0.7 63.1 %shard_map.85 = (bf16[28,8192]{1,0:T(8,128)(2,1)S(1)}, f32[28,512]{1,0:T(8,128)S(1)}) custom-call(bf16[512,1024]{1,0:T(8,128)(2,1)} %acts_hbm.1, bf16[512,1792]{1,0:T(8,128)(2,1)} %grads_hbm.1, bf16[1024,512]{1,0:T(8,128)(2,1)} %basis_hbm.1, bf16[28,8192]{1,0:T(8,128)(2,1)} %weights_hbm.1, f32[28,512]{1,0:T(8,128)} %first_hbm.1, f32[28,512]{1,0:T(8,128)} %second_hbm.1), custom_call_target="tpu_custom_call" | custom-call | tf_op jit(solution)/shard_map/pallas_call | solution.py:328
  63.8 0.0 copy-done.1
  63.8 0.0 copy-done
  63.8 0.7 %fusion = (f32[28,512]{1,0:T(8,128)}, f32[28,512]{1,0:T(8,128)}) fusion(f32[28,512]{1,0:T(8,128)S(1)} %get-tuple-element.6, f32[28,512]{1,0:T(8,128)S(1)} %copy-done.1, f32[28,512]{1,0:T(8,128)S(1)} %copy-done), kind=kLoop, calls=%fused_computation.1 | loop fusion | flops 100352 | bytes 286720 | tf_op jit(solution)/shard_map/add | solution.py:28
  64.5 0.8 %copy.10 = bf16[28,8192]{1,0:T(8,128)(2,1)} copy(bf16[28,8192]{1,0:T(8,128)(2,1)S(1)} %get-tuple-element.12) | data formatting | bytes 917504
Async XLA Ops:
  0.6 63.1 %copy-start.1 = (f32[28,512]{1,0:T(8,128)S(1)}, f32[28,512]{1,0:T(8,128)}, u32[]{:S(2)}) copy-start(f32[28,512]{1,0:T(8,128)} %second_hbm.1) | copy-start | bytes 172036
  0.6 63.1 %copy-start = (f32[28,512]{1,0:T(8,128)S(1)}, f32[28,512]{1,0:T(8,128)}, u32[]{:S(2)}) copy-start(f32[28,512]{1,0:T(8,128)} %first_hbm.1) | copy-start | bytes 172036

commit v6 on v5

--- a/solution.py
+++ b/solution.py
@@ -14,7 +14,7 @@
 adam_eps = 1e-08
 step_size = 1.0
 
-HUBS = (6, -6, 3, -3, 0)
+HUBS = (6, -6, 0, 3, -3)
 HELPERS = ((0, "row"), (1, "row"), (-1, "row"), (0, "inner"), (0, "outer"), (1, "inner"), (-1, "outer"))
 LEAVES = {6: (8, 7, 5, 6), -6: (-7, -5, -6), 3: (4, 2, 3), -3: (-4, -2, -3), 0: (1, -1, 0)}
 
@@ -85,6 +85,7 @@
         {"dp": dp_of(z + nz - 1, y_hi, core)},
     ]
     peers += [device_of(r, "outer") for r in (-1, 0, 1)]
+    peers += [{"dp": dp_of(z, 1 - y_hi, 1 - core)}]
     barrier = pltpu.get_barrier_semaphore()
     for peer in peers:
         pl.semaphore_signal(barrier, inc=1, device_id=peer, device_id_type=MESH)
@@ -198,6 +199,15 @@
             leaf[s, n] = value.astype(BF16)
         for n in members:
             e = schedule[n][1] - h
+            if h == 0:
+                for y in range(2):
+                    if e:
+                        to_hub[s, 0, e, y] = send(
+                            leaf.at[s, n, y], hub_in.at[s, i, slot(e, y)],
+                            hub_send.at[s, i, slot(e, y)], hub_recv.at[s, i, slot(e, y)],
+                            {"dp": dp_of(z - e + nz, y_hi, core)},
+                        )
+                continue
             for dy in (1, 0):
                 if e or dy:
                     y_at = (y_hi + dy) % 2
@@ -225,27 +235,41 @@
         load.wait()
     column[:, pl.ds(span // 2, 8), :] = jnp.zeros((2, 8, block), F32)
     fin = {}
-    for i, h in enumerate(HUBS):
+    home = HUBS.index(0)
+
+    def collect(i, h, v, into):
         own = schedule.index((h, h))
         for s in range(2):
-            value = leaf[s, own, y_hi].astype(F32)
+            value = leaf[s, own, (y_hi + v) % 2].astype(F32)
             for e in [o - h for o in LEAVES[h]]:
                 for dy in (0, 1):
+                    if (e or (dy and h)) and not v:
+                        to_hub[s, h, e, dy].wait()
+            for e in [o - h for o in LEAVES[h]]:
+                if h == 0:
+                    if e:
+                        value = value + hub_in[s, i, slot(e, 0) + (y_hi + v) % 2].astype(F32)
+                    continue
+                for dy in (0, 1):
                     if e or dy:
-                        to_hub[s, h, e, dy].wait()
                         value = value + hub_in[s, i, slot(e, dy)].astype(F32)
             column[s, pl.ds(0, span // 2), :] = value
             for c in range(2):
                 cut = column[s, pl.ds(c * rows, pad), :]
-                fin_out[i, c, pl.ds(s * pad, pad), :] = cut.astype(BF16)
+                fin_out[into, c, pl.ds(s * pad, pad), :] = cut.astype(BF16)
         for dc in (1, 0):
             core_at = (core + dc) % 2
-            if h or dc:
-                fin[i, dc] = send(
-                    fin_out.at[i, core_at], fin_in.at[i, dc],
-                    fin_send.at[i, dc], fin_recv.at[i, dc],
-                    {"dp": dp_of(z - h + nz, y_hi, core_at)},
+            if h or v or dc:
+                fin[into, dc] = send(
+                    fin_out.at[into, core_at], fin_in.at[into, dc],
+                    fin_send.at[into, dc], fin_recv.at[into, dc],
+                    {"dp": dp_of(z - h + nz, (y_hi + v) % 2, core_at)},
                 )
+
+    for i, h in enumerate(HUBS):
+        collect(i, h, 0, i)
+        if h == 0:
+            collect(i, 0, 1, len(HUBS))
 
     far.wait()
     swap = send(
@@ -253,14 +277,15 @@
         {"dp": dp_of(z, y_hi, 1 - core)},
     )
     for dc in range(2):
-        for i, h in enumerate(HUBS):
-            if h or dc:
+        for i in range(len(HUBS) + 1):
+            if i != home or dc:
                 fin[i, dc].wait()
         for k in range(2):
             at = pl.ds(k * pad, pad)
-            low_grad = (fin_in if dc else fin_out)[len(HUBS) - 1, 1 if dc else core, at, :].astype(F32)
-            for i in range(len(HUBS) - 1):
-                low_grad = low_grad + fin_in[i, dc, at, :].astype(F32)
+            low_grad = (fin_in if dc else fin_out)[home, 1 if dc else core, at, :].astype(F32)
+            for i in range(len(HUBS) + 1):
+                if i != home:
+                    low_grad = low_grad + fin_in[i, dc, at, :].astype(F32)
             low_grad = low_grad[:rows]
             cut = pl.ds(pl.multiple_of((2 * k + (core + dc) % 2) * block, block), block)
             moment_new, second_new = moments(first[:, cut], second[:, cut], low_grad)
@@ -349,15 +374,15 @@
             vmem((2, nz, 2, span // 2, rank // 4), BF16),
             vmem((2, hubs, 8, span // 2, rank // 4), BF16),
             vmem((2, span // 2 + 8, rank // 4), F32),
-            vmem((hubs, 2, 2 * pad, rank // 4), BF16),
-            vmem((hubs, 2, 2 * pad, rank // 4), BF16),
+            vmem((hubs + 1, 2, 2 * pad, rank // 4), BF16),
+            vmem((hubs + 1, 2, 2 * pad, rank // 4), BF16),
             vmem((peers, pad, rank), BF16),
             vmem((peers, pad, width), BF16),
             vmem((peers, pad, width), BF16),
             dma((6,)),
             dma((2, peers)), dma((2, peers)), dma((2, peers)), dma((2, peers)),
             dma((2, nz)), dma((2, nz)),
-            dma((2, hubs, 8)), dma((2, hubs, 8)), dma((hubs, 2)), dma((hubs, 2)),
+            dma((2, hubs, 8)), dma((2, hubs, 8)), dma((hubs + 1, 2)), dma((hubs + 1, 2)),
             dma((peers,)), dma((peers,)), dma((peers,)), dma((peers,)),
             pltpu.SemaphoreType.REGULAR((3, 2)),
             vmem(basis.shape, BF16),

time: 65.4 us -> 63 us (0.963)
  the two profiles are of different devices: /device:TPU:32 before, /device:TPU:1 now
where the time goes in v6:
time: 63 us; the launch traced here: 62.4 us
  Pallas kernels  60.2 us (96%)
  local copies, waits for them, and re-layouts  0.8 us (1%)
  other arithmetic  0.67 us (1%)
  between operations  0.67 us (1%)
    pallas_call x1, Pallas kernels, on_device(): pl.pallas_call(functools.partial(kernel, nz, nx, pad), out_shape=(jax.Sha...  60.2 us

profile of v6, /device:TPU:1, one launch (start us, length us, event | category | flops | bytes accessed | tf_op | source)
XLA Modules:
  0.0 62.4 jit_solution(11333389273523321847)
XLA Ops:
  0.6 0.0 copy-start.1
  0.6 0.0 copy-start
  0.7 60.2 %shard_map.85 = (bf16[28,8192]{1,0:T(8,128)(2,1)S(1)}, f32[28,512]{1,0:T(8,128)S(1)}) custom-call(bf16[512,1024]{1,0:T(8,128)(2,1)} %acts_hbm.1, bf16[512,1792]{1,0:T(8,128)(2,1)} %grads_hbm.1, bf16[1024,512]{1,0:T(8,128)(2,1)} %basis_hbm.1, bf16[28,8192]{1,0:T(8,128)(2,1)} %weights_hbm.1, f32[28,512]{1,0:T(8,128)} %first_hbm.1, f32[28,512]{1,0:T(8,128)} %second_hbm.1), custom_call_target="tpu_custom_call" | custom-call | tf_op jit(solution)/shard_map/pallas_call | solution.py:353
  60.9 0.0 copy-done.1
  60.9 0.0 copy-done
  60.9 0.7 %fusion = (f32[28,512]{1,0:T(8,128)}, f32[28,512]{1,0:T(8,128)}) fusion(f32[28,512]{1,0:T(8,128)S(1)} %get-tuple-element.6, f32[28,512]{1,0:T(8,128)S(1)} %copy-done.1, f32[28,512]{1,0:T(8,128)S(1)} %copy-done), kind=kLoop, calls=%fused_computation.1 | loop fusion | flops 100352 | bytes 286720 | tf_op jit(solution)/shard_map/add | solution.py:28
  61.6 0.8 %copy.10 = bf16[28,8192]{1,0:T(8,128)(2,1)} copy(bf16[28,8192]{1,0:T(8,128)(2,1)S(1)} %get-tuple-element.12) | data formatting | bytes 917504
Async XLA Ops:
  0.6 60.3 %copy-start.1 = (f32[28,512]{1,0:T(8,128)S(1)}, f32[28,512]{1,0:T(8,128)}, u32[]{:S(2)}) copy-start(f32[28,512]{1,0:T(8,128)} %second_hbm.1) | copy-start | bytes 172036
  0.6 60.3 %copy-start = (f32[28,512]{1,0:T(8,128)S(1)}, f32[28,512]{1,0:T(8,128)}, u32[]{:S(2)}) copy-start(f32[28,512]{1,0:T(8,128)} %first_hbm.1) | copy-start | bytes 172036

commit v7 on v6

--- a/solution.py
+++ b/solution.py
@@ -16,7 +16,11 @@
 
 HUBS = (6, -6, 0, 3, -3)
 HELPERS = ((0, "row"), (1, "row"), (-1, "row"), (0, "inner"), (0, "outer"), (1, "inner"), (-1, "outer"))
-LEAVES = {6: (8, 7, 5, 6), -6: (-7, -5, -6), 3: (4, 2, 3), -3: (-4, -2, -3), 0: (1, -1, 0)}
+NEAR = {3: (4, 2, 3), -3: (-4, -2, -3), 0: (1, -1, 0)}
+LEAVES = (
+    {6: (8, 7, 5, 6), -6: (-7, -5, -6), **NEAR},
+    {6: (7, 5, 6), -6: (-8, -7, -5, -6), **NEAR},
+)
 
 MESH = pl.DeviceIdType.MESH
 F32 = jnp.float32
@@ -162,7 +166,7 @@
     hear(2)
     tell(3)
 
-    schedule = [(h, o) for h in HUBS for o in LEAVES[h]]
+    schedule = [[(h, o) for h in HUBS for o in LEAVES[s][h]] for s in range(2)]
     block = rank // 4
     siblings, to_hub = {}, {}
 
@@ -178,7 +182,7 @@
                 halves[s, c, pl.ds(b * group, group)] = value[
                     :, :, :, c * block : (c + 1) * block
                 ].astype(BF16)
-        for n, (h, o) in enumerate(schedule):
+        for n, (h, o) in enumerate(schedule[s]):
             at = (z - o + nz) % nz
             siblings[s, n] = send(
                 halves.at[s, 1 - core, at], sibling_in.at[s, n],
@@ -186,19 +190,19 @@
             )
 
     def slot(e, dy):
-        return (e + 1) * 2 + dy
+        return (e + 2) * 2 + dy
 
     def scatter(s, h):
         i = HUBS.index(h)
-        members = [n for n in range(nz) if schedule[n][0] == h]
+        members = [n for n in range(nz) if schedule[s][n][0] == h]
         for n in members:
             siblings[s, n].wait()
         for n in members:
-            at = (z - schedule[n][1] + nz) % nz
+            at = (z - schedule[s][n][1] + nz) % nz
             value = halves[s, core, at].astype(F32) + sibling_in[s, n].astype(F32)
             leaf[s, n] = value.astype(BF16)
         for n in members:
-            e = schedule[n][1] - h
+            e = schedule[s][n][1] - h
             if h == 0:
                 for y in range(2):
                     if e:
@@ -238,14 +242,14 @@
     home = HUBS.index(0)
 
     def collect(i, h, v, into):
-        own = schedule.index((h, h))
         for s in range(2):
+            own = schedule[s].index((h, h))
             value = leaf[s, own, (y_hi + v) % 2].astype(F32)
-            for e in [o - h for o in LEAVES[h]]:
+            for e in [o - h for o in LEAVES[s][h]]:
                 for dy in (0, 1):
                     if (e or (dy and h)) and not v:
                         to_hub[s, h, e, dy].wait()
-            for e in [o - h for o in LEAVES[h]]:
+            for e in [o - h for o in LEAVES[s][h]]:
                 if h == 0:
                     if e:
                         value = value + hub_in[s, i, slot(e, 0) + (y_hi + v) % 2].astype(F32)
@@ -372,7 +376,7 @@
             vmem((2, 2, nz, 2, span // 2, rank // 4), BF16),
             vmem((2, nz, 2, span // 2, rank // 4), BF16),
             vmem((2, nz, 2, span // 2, rank // 4), BF16),
-            vmem((2, hubs, 8, span // 2, rank // 4), BF16),
+            vmem((2, hubs, 10, span // 2, rank // 4), BF16),
             vmem((2, span // 2 + 8, rank // 4), F32),
             vmem((hubs + 1, 2, 2 * pad, rank // 4), BF16),
             vmem((hubs + 1, 2, 2 * pad, rank // 4), BF16),
@@ -382,7 +386,7 @@
             dma((6,)),
             dma((2, peers)), dma((2, peers)), dma((2, peers)), dma((2, peers)),
             dma((2, nz)), dma((2, nz)),
-            dma((2, hubs, 8)), dma((2, hubs, 8)), dma((hubs + 1, 2)), dma((hubs + 1, 2)),
+            dma((2, hubs, 10)), dma((2, hubs, 10)), dma((hubs + 1, 2)), dma((hubs + 1, 2)),
             dma((peers,)), dma((peers,)), dma((peers,)), dma((peers,)),
             pltpu.SemaphoreType.REGULAR((3, 2)),
             vmem(basis.shape, BF16),

time: 63 us -> 62.8 us (level)
  no operation moved by 1% of the time
where the time goes in v7:
time: 62.8 us; the launch traced here: 62.6 us
  Pallas kernels  60.5 us (96%)
  local copies, waits for them, and re-layouts  0.8 us (1%)
  other arithmetic  0.67 us (1%)
  between operations  0.67 us (1%)
    pallas_call x1, Pallas kernels, on_device(): pl.pallas_call(functools.partial(kernel, nz, nx, pad), out_shape=(jax.Sha...  60.5 us

profile of v7, /device:TPU:1, one launch (start us, length us, event | category | flops | bytes accessed | tf_op | source)
XLA Modules:
  0.0 62.6 jit_solution(4307214839621824086)
XLA Ops:
  0.6 0.0 copy-start.1
  0.6 0.0 copy-start
  0.7 60.5 %shard_map.85 = (bf16[28,8192]{1,0:T(8,128)(2,1)S(1)}, f32[28,512]{1,0:T(8,128)S(1)}) custom-call(bf16[512,1024]{1,0:T(8,128)(2,1)} %acts_hbm.1, bf16[512,1792]{1,0:T(8,128)(2,1)} %grads_hbm.1, bf16[1024,512]{1,0:T(8,128)(2,1)} %basis_hbm.1, bf16[28,8192]{1,0:T(8,128)(2,1)} %weights_hbm.1, f32[28,512]{1,0:T(8,128)} %first_hbm.1, f32[28,512]{1,0:T(8,128)} %second_hbm.1), custom_call_target="tpu_custom_call" | custom-call | tf_op jit(solution)/shard_map/pallas_call | solution.py:357
  61.1 0.0 copy-done.1
  61.1 0.0 copy-done
  61.1 0.7 %fusion = (f32[28,512]{1,0:T(8,128)}, f32[28,512]{1,0:T(8,128)}) fusion(f32[28,512]{1,0:T(8,128)S(1)} %get-tuple-element.6, f32[28,512]{1,0:T(8,128)S(1)} %copy-done.1, f32[28,512]{1,0:T(8,128)S(1)} %copy-done), kind=kLoop, calls=%fused_computation.1 | loop fusion | flops 100352 | bytes 286720 | tf_op jit(solution)/shard_map/add | solution.py:32
  61.8 0.8 %copy.10 = bf16[28,8192]{1,0:T(8,128)(2,1)} copy(bf16[28,8192]{1,0:T(8,128)(2,1)S(1)} %get-tuple-element.12) | data formatting | bytes 917504
Async XLA Ops:
  0.6 60.5 %copy-start.1 = (f32[28,512]{1,0:T(8,128)S(1)}, f32[28,512]{1,0:T(8,128)}, u32[]{:S(2)}) copy-start(f32[28,512]{1,0:T(8,128)} %second_hbm.1) | copy-start | bytes 172036
  0.6 60.5 %copy-start = (f32[28,512]{1,0:T(8,128)S(1)}, f32[28,512]{1,0:T(8,128)}, u32[]{:S(2)}) copy-start(f32[28,512]{1,0:T(8,128)} %first_hbm.1) | copy-start | bytes 172036
